TPU v7x, 32 devices: a whole 2x2x4 slice. The times are simulated.
32 devices in a mesh: slab: 2 (over x), scan: 8 (over z, y), mz: 2 (over core).
Axes of the slice: x: 2, y: 2, z: 4, core: 2. Of those that a mesh axis runs over, the one named last changes fastest.
Arguments:
- spectra: bfloat16 [12288, 8192], P('mz', ('slab', 'scan')), parts along dimension 1, may hold values from 0 to 1
- templates: bfloat16 [2, 12288, 512], P('mz', ('slab', 'scan')), parts along dimension 1, may hold values from 0 to 2
- activations: float32 [64, 8192], P(None, ('slab', 'scan')), parts along dimension 1, may hold values from 0 to 1
- h_rate: float32 [64], replicated, may hold values from 0.02 to 0.08
- w_rate: float32 [64], replicated, may hold values from 0.2 to 0.8
Outputs:
- new_activations: float32 [64, 8192], P(None, ('slab', 'scan')), parts along dimension 1
- new_templates: bfloat16 [2, 12288, 512], P('mz', ('slab', 'scan')), parts along dimension 1
There are 2 independent parts, one for each index of `slab`. A program takes and returns all parts, laid end to end along the dimension named above; an argument that names none is the same for every part. Nothing has to cross between parts.
All inputs are finite; a program needn't handle non-finite values.
Results may differ from a plain program's by a relative error of at most 0.00082.
Values may be sent and summed in bfloat16 or wider, within the bound.
A program may use at most 128 MiB of HBM per device.

v0:
```python
import jax
import jax.numpy as jnp
from jax import lax
from jax.sharding import PartitionSpec as P

K = 64
LAGS = 8
LAG = 64
SPAN = 448


def shifted(x, axis, by):
    size = lax.axis_size(axis)
    pairs = [(i, i + by) for i in range(size) if 0 <= i + by < size]
    return lax.ppermute(x, axis, pairs)


def lagged(hb):
    width = hb.shape[1]
    tail = shifted(hb[:, width - SPAN :], "scan", 1)
    extended = jnp.concatenate([tail, hb], 1)
    return jnp.concatenate(
        [extended[:, SPAN - l * LAG : SPAN - l * LAG + width] for l in range(LAGS)], 0
    )


def lag_total(prods, count):
    width = prods.shape[1]
    after = shifted(prods[:, :SPAN], "scan", -1)
    extended = jnp.concatenate([prods, after], 1)
    total = extended[0:count, 0:width]
    for l in range(1, LAGS):
        total = total + extended[l * count : (l + 1) * count, l * LAG : l * LAG + width]
    return total


def per_device(spectra, templates, activations, h_rate, w_rate):
    scale = 1.0 / (LAGS * K)
    own_rows = templates.reshape(templates.shape[1], templates.shape[2])
    weights = lax.all_gather(own_rows, "scan", axis=0, tiled=True)
    data = spectra.astype(jnp.float32)
    stack = lagged(activations.astype(jnp.bfloat16))
    recon = scale * jnp.dot(weights, stack, preferred_element_type=jnp.float32)
    resid = (recon - data).astype(jnp.bfloat16)
    prods = lax.dot_general(
        weights, resid, (((0,), (0,)), ((), ())), preferred_element_type=jnp.float32
    )
    summed = lax.psum(prods, "mz")
    grad_h = scale * lag_total(summed, K)
    new_h = jnp.maximum(activations - h_rate[:, None] * grad_h, 0.0)
    new_hb = new_h.astype(jnp.bfloat16)
    stack_new = lagged(new_hb)
    recon_new = scale * jnp.dot(weights, stack_new, preferred_element_type=jnp.float32)
    resid_new = (recon_new - data).astype(jnp.bfloat16)
    gathered_rows = lax.all_to_all(resid_new, "scan", split_axis=0, concat_axis=1, tiled=True)
    all_h = lax.all_gather(new_hb, "scan", axis=1, tiled=True)
    total = all_h.shape[1]
    padded = jnp.pad(all_h, ((0, 0), (SPAN, 0)))
    full_stack = jnp.concatenate(
        [padded[:, SPAN - l * LAG : SPAN - l * LAG + total] for l in range(LAGS)], 0
    )
    grad_w = scale * lax.dot_general(
        gathered_rows, full_stack, (((1,), (1,)), ((), ())), preferred_element_type=jnp.float32
    )
    rates = jnp.tile(w_rate, LAGS)[None, :]
    new_w = jnp.maximum(own_rows.astype(jnp.float32) - rates * grad_w, 0.0).astype(jnp.bfloat16)
    return (new_h, new_w.reshape(templates.shape))


def solution(mesh):
    placed = (
        P("mz", ("slab", "scan")),
        P("mz", ("slab", "scan"), None),
        P(None, ("slab", "scan")),
        P(),
        P(),
    )
    return jax.shard_map(
        per_device,
        mesh=mesh,
        in_specs=placed,
        out_specs=(P(None, ("slab", "scan")), P("mz", ("slab", "scan"), None)),
        check_vma=False,
    )
```

profile of v0, /device:TPU:0, one launch (start us, length us, event | category | flops | bytes accessed | tf_op | source)
XLA Modules:
  0.0 383.8 jit_solution(8813983667833982358)
XLA Ops:
  7.2 0.0 all-gather.3.cloned.1.call-start
  7.2 0.7 all-gather.3.cloned.1.call-update
  7.9 0.0 all-reduce.3.cloned.1.call-start
  7.9 0.9 constant_dynamic-update-slice_fusion
  8.9 0.1 slice.129
  9.0 4.9 %collective-permute-start = (bf16[64,448]{1,0:T(8,128)(2,1)S(1)}, bf16[64,448]{1,0:T(8,128)(2,1)S(1)}, u32[]{:S(2)}, u32[]{:S(2)}) collective-permute-start(bf16[64,448]{1,0:T(8,128)(2,1)S(1)} %slice.129), channel_id=1, source_target_pairs={{0,2},{2,4},{4,6},{6,8},{8,10},{10,12},{12,14},{1,3},{3,5},{5,7},{... | collective-permute-start | bytes 172040 | tf_op jit(solution)/shard_map/ppermute | solution.py:15
  13.8 8.8 %copy.10 = bf16[6144,512]{0,1:T(8,128)(2,1)} copy(bf16[6144,512]{1,0:T(8,128)(2,1)} %param.5) | data formatting | bytes 12582912 | tf_op args[0]
  22.6 0.0 collective-permute-done
  22.6 0.1 fusion.28
  22.7 0.1 fusion.30
  22.8 0.1 fusion.32
  22.9 0.1 fusion.34
  23.0 0.1 fusion.36
  23.1 0.1 fusion.26
  23.2 0.1 fusion.37
  23.2 0.0 copy-start
  23.2 0.0 copy-start.1
  23.2 88.7 %all-gather.3.cloned.1.call-done = bf16[1,6144,512]{2,1,0:T(8,128)(2,1)} async-done(((bf16[1,768,512]{2,1,0:T(8,128)(2,1)}), bf16[1,6144,512]{2,1,0:T(8,128)(2,1)}) %all-gather.3.cloned.1.call-update) | async-done | bytes 6291472 | tf_op jit(solution)/shard_map/all_gather | solution.py:40
  111.9 14.2 %fusion.10 = f32[512,512]{0,1:T(8,128)} fusion(bf16[1,6144,512]{2,1,0:T(8,128)(2,1)} %all-gather.3.cloned.1.call-done, bf16[6144,512]{0,1:T(8,128)(2,1)} %copy.10, bf16[512,512]{1,0:T(8,128)(2,1)S(1)} %fusion.37), kind=kOutput, calls=%fused_computation.12 | convolution fusion | flops 6455033856 | bytes 14155776 | tf_op jit(solution)/shard_map/dot_general | solution.py:45
  126.1 0.0 all-reduce.3.cloned.1.call-update
  126.1 17.9 %all-reduce.3.cloned.1.call-done = f32[512,512]{0,1:T(8,128)} async-done(((f32[512,512]{0,1:T(8,128)}), f32[512,512]{0,1:T(8,128)}) %all-reduce.3.cloned.1.call-update) | async-done | bytes 1048592 | tf_op jit(solution)/shard_map/psum | solution.py:48
  144.1 1.2 slice.143
  145.3 1.3 collective-permute-start.1
  146.6 0.0 copy-done
  146.6 0.1 copy.11
  146.7 0.0 copy-done.1
  146.8 1.3 constant_dynamic-update-slice_fusion.2
  148.1 21.7 %collective-permute-done.1 = f32[512,448]{0,1:T(8,128)S(1)} collective-permute-done((f32[512,448]{0,1:T(8,128)S(1)}, f32[512,448]{0,1:T(8,128)S(1)}, u32[]{:S(2)}, u32[]{:S(2)}) %collective-permute-start.1) | collective-permute-done | bytes 917536 | tf_op jit(solution)/shard_map/ppermute | solution.py:15
  169.7 0.1 constant_dynamic-update-slice_fusion.1
  169.8 1.3 fusion.39
  171.1 4.5 %collective-permute-start.2 = (bf16[64,448]{0,1:T(8,128)(2,1)S(1)}, bf16[64,448]{0,1:T(8,128)(2,1)S(1)}, u32[]{:S(2)}, u32[]{:S(2)}) collective-permute-start(bf16[64,448]{0,1:T(8,128)(2,1)S(1)} %slice.151), channel_id=1, source_target_pairs={{0,2},{2,4},{4,6},{6,8},{8,10},{10,12},{12,14},{1,3},{3,5},{5,7},{... | collective-permute-start | bytes 172040 | tf_op jit(solution)/shard_map/ppermute | solution.py:15
  175.7 2.3 collective-permute-done.2
  178.0 0.1 pad_maximum_fusion
  178.2 0.5 concatenate.22
  178.7 7.5 %fusion.1 = bf16[6144,512]{0,1:T(8,128)(2,1)S(1)} fusion(bf16[6144,512]{0,1:T(8,128)(2,1)} %copy.10, bf16[512,512]{0,1:T(8,128)(2,1)S(1)} %concatenate.22, bf16[1,6144,512]{2,1,0:T(8,128)(2,1)} %all-gather.3.cloned.1.call-done), kind=kOutput, calls=%fused_computation.3 | convolution fusion | flops 3233808384 | bytes 19398656 | tf_op jit(solution)/shard_map/dot_general | solution.py:53
  186.1 3.1 copy.16
  189.2 0.0 copy-start.2
  189.2 5.7 %all-to-all-start = ((bf16[8,768,512]{1,2,0:T(8,128)(2,1)}), bf16[8,768,512]{1,2,0:T(8,128)(2,1)}, u32[]{:S(2)}, u32[]{:S(2)}) async-start(bf16[8,768,512]{1,2,0:T(8,128)(2,1)} %bitcast.39), calls=%async_computation | async-start | bytes 12582912 | tf_op jit(solution)/shard_map/all_to_all | solution.py:55
  194.9 0.0 copy-done.2
  194.9 0.1 mul.49
  195.0 0.8 copy.13
  195.8 158.6 %all_gather.7 = bf16[64,4096]{0,1:T(8,128)(2,1)S(1)} all-gather(bf16[64,512]{0,1:T(8,128)(2,1)S(1)} %get-tuple-element.6), channel_id=1, replica_groups=mesh['slab'=2,'scan'=8,'mz'=2] {'scan'}, dimensions={1}, use_global_device_ids=true | all-gather | bytes 589824 | tf_op jit(solution)/shard_map/all_gather | solution.py:56
  354.3 3.6 pad_slice_fusion
  357.9 10.5 %concatenate.23 = bf16[512,4096]{0,1:T(8,128)(2,1)} concatenate(bf16[64,4096]{0,1:T(8,128)(2,1)S(1)} %all_gather.7, bf16[64,4096]{0,1:T(8,128)(2,1)} %get-tuple-element.16, bf16[64,4096]{0,1:T(8,128)(2,1)S(1)} %get-tuple-element.11, bf16[64,4096]{0,1:T(8,128)(2,1)} %get-tuple-element.12, bf16[64,4096]{0,1:T(8,128)(2,1)} %get-tuple-element.13, ...), dimensions={0} | concatenate | bytes 8388608 | tf_op jit(solution)/shard_map/concatenate | solution.py:59
  368.4 0.0 all-to-all-done
  368.4 8.5 %fusion.15 = bf16[1,768,512]{2,1,0:T(8,128)(2,1)} fusion(bf16[768,4096]{0,1:T(8,128)(2,1)} %bitcast.6, bf16[512,4096]{0,1:T(8,128)(2,1)} %concatenate.23, bf16[1,768,512]{2,1,0:T(8,128)(2,1)} %param.6, f32[512]{0:T(512)S(1)} %mul.49), kind=kOutput, calls=%fused_computation.13 | convolution fusion | flops 3223191552 | bytes 12060672 | tf_op jit(solution)/shard_map/dot_general | solution.py:62
  (4 shorter events, 0.0 us)
Async XLA Ops:
  7.2 104.8 %all-gather.3.cloned.1.call-start = ((), (), s32[]{:S(2)}) async-start(), calls=%async_computation.2 | async-start | bytes 7077888 | tf_op jit(solution)/shard_map/all_gather | solution.py:40
  7.9 136.2 %all-reduce.3.cloned.1.call-start = ((), (), s32[]{:S(2)}) async-start(), calls=%async_computation.1 | async-start | bytes 2097152 | tf_op jit(solution)/shard_map/psum | solution.py:48
  9.0 13.7 %collective-permute-start = (bf16[64,448]{1,0:T(8,128)(2,1)S(1)}, bf16[64,448]{1,0:T(8,128)(2,1)S(1)}, u32[]{:S(2)}, u32[]{:S(2)}) collective-permute-start(bf16[64,448]{1,0:T(8,128)(2,1)S(1)} %slice.129), channel_id=1, source_target_pairs={{0,2},{2,4},{4,6},{6,8},{8,10},{10,12},{12,14},{1,3},{3,5},{5,7},{... | collective-permute-start | bytes 172040 | tf_op jit(solution)/shard_map/ppermute | solution.py:15
  23.2 123.4 %copy-start = (f32[64,512]{1,0:T(8,128)S(1)}, f32[64,512]{1,0:T(8,128)}, u32[]{:S(2)}) copy-start(f32[64,512]{1,0:T(8,128)} %param.7) | copy-start | bytes 393220
  23.2 123.5 %copy-start.1 = (f32[64]{0:T(128)S(1)}, f32[64]{0:T(128)}, u32[]{:S(2)}) copy-start(f32[64]{0:T(128)} %param.8) | copy-start | bytes 772
  145.3 24.4 %collective-permute-start.1 = (f32[512,448]{0,1:T(8,128)S(1)}, f32[512,448]{0,1:T(8,128)S(1)}, u32[]{:S(2)}, u32[]{:S(2)}) collective-permute-start(f32[512,448]{0,1:T(8,128)S(1)} %slice.143), channel_id=1, source_target_pairs={{2,0},{4,2},{6,4},{8,6},{10,8},{12,10},{14,12},{3,1},{5,3},{7,5},{... | collective-permute-start | bytes 2752520 | tf_op jit(solution)/shard_map/ppermute | solution.py:15
  171.1 6.9 %collective-permute-start.2 = (bf16[64,448]{0,1:T(8,128)(2,1)S(1)}, bf16[64,448]{0,1:T(8,128)(2,1)S(1)}, u32[]{:S(2)}, u32[]{:S(2)}) collective-permute-start(bf16[64,448]{0,1:T(8,128)(2,1)S(1)} %slice.151), channel_id=1, source_target_pairs={{0,2},{2,4},{4,6},{6,8},{8,10},{10,12},{12,14},{1,3},{3,5},{5,7},{... | collective-permute-start | bytes 172040 | tf_op jit(solution)/shard_map/ppermute | solution.py:15
  189.2 5.7 %copy-start.2 = (f32[64]{0:T(128)S(1)}, f32[64]{0:T(128)}, u32[]{:S(2)}) copy-start(f32[64]{0:T(128)} %param.9) | copy-start | bytes 772
  189.2 179.3 %all-to-all-start = ((bf16[8,768,512]{1,2,0:T(8,128)(2,1)}), bf16[8,768,512]{1,2,0:T(8,128)(2,1)}, u32[]{:S(2)}, u32[]{:S(2)}) async-start(bf16[8,768,512]{1,2,0:T(8,128)(2,1)} %bitcast.39), calls=%async_computation | async-start | bytes 12582912 | tf_op jit(solution)/shard_map/all_to_all | solution.py:55
Sparse Core Ops, SparseCore 0:
  10.2 101.7 all-gather.2
  126.2 17.7 all-reduce.2
where the time goes:
time: 385 us; the launch traced here: 384 us
  blocking collectives  159 us (41%)
  waiting for transfers between devices  131 us (34%)
  local copies, waits for them, and re-layouts  30.1 us (8%)
  matrix products  30.1 us (8%)
  starting transfers between devices  16.5 us (4%)
  between operations  14.2 us (4%)
    all_gather x1, blocking collectives, per_device(): all_h = lax.all_gather(new_hb, 'scan', axis=1, tiled=True)  159 us
    all_gather x1, waiting for transfers between devices, per_device(): weights = lax.all_gather(own_rows, 'scan', axis=0, tiled=True)  88.7 us
    ppermute x3, waiting for transfers between devices, shifted(): return lax.ppermute(x, axis, pairs)  24 us
    psum x1, waiting for transfers between devices, per_device(): summed = lax.psum(prods, 'mz')  17.9 us
    dot_general x1, matrix products, per_device(): lax.dot_general(weights, resid, (((0,), (0,)), ((), ())), preferred_eleme...  14.2 us
    unnamed x10, local copies, waits for them, and re-layouts  11 us
    ppermute x3, starting transfers between devices, shifted(): return lax.ppermute(x, axis, pairs)  10.7 us
    concatenate x1, local copies, waits for them, and re-layouts, per_device(): jnp.concatenate([padded[:, SPAN - l * LAG:SPAN - l * LAG + total] for l i...  10.5 us
  transfers between devices with their start and end apart: 6, of which 4 were waited for; matrix products, arithmetic and copies ran while one was open for 7% of the time, Pallas kernels for 0%

commit v1 on v0

v1 whole, which is shorter than its diff:
```python
import functools

import jax
import jax.numpy as jnp
from jax import lax
from jax.experimental import pallas as pl
from jax.experimental.pallas import tpu as pltpu
from jax.sharding import PartitionSpec as P

K = 64
LAGS = 8
LAG = 64
LANES = 128
F32 = jnp.float32
BF16 = jnp.bfloat16
MESH = pl.DeviceIdType.MESH


def crossed(a, b, n):
    out, bit = 0, 1
    while bit < n:
        out = out + bit * ((a // bit + b // bit) % 2)
        bit *= 2
    return out


def kernel(
    n, chunks, spectra, w_ref, act_ref, h_rate, w_rate, h_out, w_out,
    sbuf, hraw, stack, gacc, gfin, from_core, gsum, from_scan, nh, hn, total_w,
    own_sem, s_send, s_recv, h_send, h_recv, a_sem, b_send, b_recv, c_send, c_recv, d_sem, e_sem,
):
    rows, width = sbuf.shape[1], sbuf.shape[2]
    half = width // 2
    step = rows // chunks
    scale = 1.0 / (LAGS * K)
    i = lax.axis_index("scan")
    mz = lax.axis_index("mz")
    other = 1 - mz
    two = n & (n - 1) == 0

    def to(d):
        return crossed(i, d, n) if two else lax.rem(i + d, n)

    def source(d):
        return crossed(i, d, n) if two else lax.rem(i + n - d, n)

    def each(body, start=1):
        def run(d, carry):
            body(d)
            return carry

        lax.fori_loop(start, n, run, 0)

    barrier = pltpu.get_barrier_semaphore()
    each(lambda d: pl.semaphore_signal(barrier, inc=1, device_id={"scan": to(d)}, device_id_type=MESH))
    pl.semaphore_signal(barrier, inc=1, device_id={"mz": other}, device_id_type=MESH)
    hraw[i] = act_ref[...].astype(BF16)
    pl.semaphore_wait(barrier, n)

    def send_h(d):
        return pltpu.make_async_remote_copy(
            src_ref=hraw.at[i], dst_ref=hraw.at[i], send_sem=h_send.at[d], recv_sem=h_recv.at[i],
            device_id={"scan": to(d)}, device_id_type=MESH,
        )

    def land_h(d):
        return pltpu.make_async_remote_copy(
            src_ref=hraw.at[source(d)], dst_ref=hraw.at[source(d)], send_sem=h_send.at[d],
            recv_sem=h_recv.at[source(d)], device_id={"scan": to(d)}, device_id_type=MESH,
        )

    def send_s(c, d):
        return pltpu.make_async_remote_copy(
            src_ref=spectra.at[pl.ds(pl.multiple_of(to(d) * rows + c * step, step), step), :],
            dst_ref=sbuf.at[i, pl.ds(c * step, step), :],
            send_sem=s_send.at[c, d], recv_sem=s_recv.at[c, i],
            device_id={"scan": to(d)}, device_id_type=MESH,
        )

    def land_s(c, d):
        return pltpu.make_async_remote_copy(
            src_ref=spectra.at[pl.ds(c * step, step), :],
            dst_ref=sbuf.at[source(d), pl.ds(c * step, step), :],
            send_sem=s_send.at[c, d], recv_sem=s_recv.at[c, source(d)],
            device_id={"scan": to(d)}, device_id_type=MESH,
        )

    own = pltpu.make_async_copy(
        spectra.at[pl.ds(pl.multiple_of(i * rows, rows), rows), :], sbuf.at[i], own_sem
    )
    own.start()
    each(lambda d: send_h(d).start())
    for c in range(chunks):
        each(lambda e, c=c: send_s(c, n - e).start())

    gacc[...] = jnp.zeros_like(gacc)
    each(lambda d: land_h(d).wait_recv())

    def build(block):
        def one(j):
            now = block(j).astype(F32)
            before = jnp.where(j > 0, block(jnp.maximum(j - 1, 0)).astype(F32), 0.0)
            ext = jnp.concatenate([before, now], 1)
            odd = pltpu.roll(ext, LAG, 1)
            for l in range(LAGS):
                start = width - LANES * (l // 2)
                part = (odd if l % 2 else ext)[:, start : start + width]
                stack[j, l * K : (l + 1) * K, :] = part.astype(BF16)

        each(one, 0)

    build(lambda j: hraw[j])
    own.wait()

    def residual(c, j):
        at = pl.ds(c * step, step)
        recon = jnp.dot(w_ref[at, :], stack[j], preferred_element_type=F32)
        return (scale * recon - sbuf[j, at, :].astype(F32)).astype(BF16)

    groups = width // LANES

    def unit(c, j):
        prods = lax.dot_general(
            w_ref[pl.ds(c * step, step), :], residual(c, j), (((0,), (0,)), ((), ())),
            preferred_element_type=F32,
        )
        for odd in range(2):
            for q in range(1 - groups, groups):
                terms = []
                for m in range(LAGS // 2):
                    if 0 <= q + m < groups:
                        l = 2 * m + odd
                        terms.append(
                            prods[l * K : (l + 1) * K, (q + m) * LANES : (q + m + 1) * LANES]
                        )
                if not terms:
                    continue
                block = j + 1 if q >= 0 else j
                at = (q % groups) * LANES
                gacc[odd, block, :, at : at + LANES] += functools.reduce(lambda a, b: a + b, terms)

    for c in range(chunks):
        unit(c, i)

        def arrived(d, c=c):
            land_s(c, d).wait_recv()
            unit(c, source(d))

        each(arrived)

    def finish(j):
        after = jnp.concatenate([gacc[1, j + 1], gacc[1, j + 2]], 1)
        g = gacc[0, j + 1] + pltpu.roll(after, 2 * width - LAG, 1)[:, :width]
        gfin[0, j] = g[:, :half]
        gfin[1, j] = g[:, half:]

    each(finish, 0)

    a_copy = pltpu.make_async_remote_copy(
        src_ref=gfin.at[other], dst_ref=from_core, send_sem=a_sem.at[0], recv_sem=a_sem.at[1],
        device_id={"mz": other}, device_id_type=MESH,
    )
    a_copy.start()
    a_copy.wait_recv()

    def add_core(j):
        gsum[j] = gfin[mz, j] + from_core[j]

    each(add_core, 0)

    def send_g(d):
        return pltpu.make_async_remote_copy(
            src_ref=gsum.at[to(d)], dst_ref=from_scan.at[i], send_sem=b_send.at[d],
            recv_sem=b_recv.at[i], device_id={"scan": to(d)}, device_id_type=MESH,
        )

    def land_g(d):
        return pltpu.make_async_remote_copy(
            src_ref=gsum.at[to(d)], dst_ref=from_scan.at[source(d)], send_sem=b_send.at[d],
            recv_sem=b_recv.at[source(d)], device_id={"scan": to(d)}, device_id_type=MESH,
        )

    each(lambda e: send_g(n - e).start())

    def add_scan(d, total):
        land_g(d).wait_recv()
        return total + from_scan[source(d)]

    grad = scale * lax.fori_loop(1, n, add_scan, gsum[i])
    act = act_ref[...]
    act = jnp.where(mz == 0, act[:, :half], act[:, half:])
    new_h = jnp.maximum(act - h_rate[...] * grad, 0.0)
    nh[mz] = new_h
    hn[mz, i] = new_h.astype(BF16)

    def send_n(d):
        return pltpu.make_async_remote_copy(
            src_ref=hn.at[mz, i], dst_ref=hn.at[mz, i], send_sem=c_send.at[d],
            recv_sem=c_recv.at[i], device_id={"scan": to(d)}, device_id_type=MESH,
        )

    def land_n(d):
        return pltpu.make_async_remote_copy(
            src_ref=hn.at[mz, source(d)], dst_ref=hn.at[mz, source(d)], send_sem=c_send.at[d],
            recv_sem=c_recv.at[source(d)], device_id={"scan": to(d)}, device_id_type=MESH,
        )

    each(lambda e: send_n(n - e).start())
    e_copy = pltpu.make_async_remote_copy(
        src_ref=nh.at[mz], dst_ref=nh.at[mz], send_sem=e_sem.at[0], recv_sem=e_sem.at[1],
        device_id={"mz": other}, device_id_type=MESH,
    )
    e_copy.start()
    each(lambda d: land_n(d).wait_recv())
    d_copy = pltpu.make_async_remote_copy(
        src_ref=hn.at[mz], dst_ref=hn.at[mz], send_sem=d_sem.at[0], recv_sem=d_sem.at[1],
        device_id={"mz": other}, device_id_type=MESH,
    )
    d_copy.start()
    e_back = pltpu.make_async_remote_copy(
        src_ref=nh.at[other], dst_ref=nh.at[other], send_sem=e_sem.at[0], recv_sem=e_sem.at[1],
        device_id={"mz": other}, device_id_type=MESH,
    )
    e_back.wait_recv()
    h_out[...] = jnp.concatenate([nh[0], nh[1]], 1)
    d_back = pltpu.make_async_remote_copy(
        src_ref=hn.at[other], dst_ref=hn.at[other], send_sem=d_sem.at[0], recv_sem=d_sem.at[1],
        device_id={"mz": other}, device_id_type=MESH,
    )
    d_back.wait_recv()
    build(lambda j: jnp.concatenate([hn[0, j], hn[1, j]], 1))

    for c in range(chunks):
        total_w[...] = jnp.zeros_like(total_w)

        def add_w(j, c=c):
            total_w[...] += lax.dot_general(
                residual(c, j), stack[j], (((1,), (1,)), ((), ())), preferred_element_type=F32
            )

        each(add_w, 0)
        at = pl.ds(c * step, step)
        moved = w_ref[at, :].astype(F32) - w_rate[...] * (scale * total_w[...])
        w_out[at, :] = jnp.maximum(moved, 0.0).astype(BF16)

    each(lambda d: send_h(d).wait_send())
    for c in range(chunks):
        each(lambda d, c=c: send_s(c, d).wait_send())
    each(lambda d: send_g(d).wait_send())
    each(lambda d: send_n(d).wait_send())
    a_copy.wait_send()
    d_copy.wait_send()
    e_copy.wait_send()


def per_device(n, spectra, templates, activations, h_rate, w_rate):
    rows, cols = templates.shape[1], templates.shape[2]
    width = spectra.shape[1]
    half = width // 2
    chunks = rows // 256 if rows % 256 == 0 else 1
    vmem = pl.BlockSpec(memory_space=pltpu.VMEM)
    dma = pltpu.SemaphoreType.DMA
    new_h, new_w = pl.pallas_call(
        functools.partial(kernel, n, chunks),
        out_shape=(
            jax.ShapeDtypeStruct(activations.shape, F32),
            jax.ShapeDtypeStruct((rows, cols), BF16),
        ),
        in_specs=[pl.BlockSpec(memory_space=pl.ANY), vmem, vmem, vmem, vmem],
        out_specs=(vmem, vmem),
        scratch_shapes=[
            pltpu.VMEM((n, rows, width), BF16),
            pltpu.VMEM((n, K, width), BF16),
            pltpu.VMEM((n, cols, width), BF16),
            pltpu.VMEM((2, n + 2, K, width), F32),
            pltpu.VMEM((2, n, K, half), F32),
            pltpu.VMEM((n, K, half), F32),
            pltpu.VMEM((n, K, half), F32),
            pltpu.VMEM((n, K, half), F32),
            pltpu.VMEM((2, K, half), F32),
            pltpu.VMEM((2, n, K, half), BF16),
            pltpu.VMEM((rows // chunks, cols), F32),
            dma,
            dma((chunks, n)),
            dma((chunks, n)),
            dma((n,)),
            dma((n,)),
            dma((2,)),
            dma((n,)),
            dma((n,)),
            dma((n,)),
            dma((n,)),
            dma((2,)),
            dma((2,)),
        ],
        compiler_params=pltpu.CompilerParams(
            collective_id=0, has_side_effects=True, vmem_limit_bytes=56 * 1024 * 1024
        ),
        cost_estimate=pl.CostEstimate(
            flops=8 * n * rows * cols * width, bytes_accessed=4 * n * rows * width, transcendentals=0
        ),
    )(
        spectra,
        templates.reshape(rows, cols),
        activations,
        h_rate[:, None],
        jnp.tile(w_rate, LAGS)[None, :],
    )
    return new_h, new_w.reshape(templates.shape)


def solution(mesh):
    placed = (
        P("mz", ("slab", "scan")),
        P("mz", ("slab", "scan"), None),
        P(None, ("slab", "scan")),
        P(),
        P(),
    )
    return jax.shard_map(
        functools.partial(per_device, mesh.shape["scan"]),
        mesh=mesh,
        in_specs=placed,
        out_specs=(P(None, ("slab", "scan")), P("mz", ("slab", "scan"), None)),
        check_vma=False,
    )
```

time: 385 us -> 205 us (0.53)
  Pallas kernels: 0 us -> 198 us
  blocking collectives: 159 us -> 0 us
  waiting for transfers between devices: 131 us -> 0 us
  matrix products: 30.1 us -> 0 us
  local copies, waits for them, and re-layouts: 30.1 us -> 6.3 us
  starting transfers between devices: 16.5 us -> 0 us
  between operations: 14.2 us -> 0.64 us
    pallas_call x0 -> x1, Pallas kernels: none -> 198 us  [per_device(): pl.pallas_call(functools.partial(kernel, n, chunks), out_shape=(jax.Shape...]
    all_gather x1 -> x0, blocking collectives: 159 us -> none  [per_device(): all_h = lax.all_gather(new_hb, 'scan', axis=1, tiled=True)]
    all_gather x1 -> x0, waiting for transfers between devices: 88.7 us -> none  [per_device(): weights = lax.all_gather(own_rows, 'scan', axis=0, tiled=True)]
    dot_general x3 -> x0, matrix products: 30.1 us -> none  [the longest x1 14.2 us: per_device(): lax.dot_general(weights, resid, (((0,), (0,)), ((), ())), preferred_eleme...]
    ppermute x3 -> x0, waiting for transfers between devices: 24 us -> none  [shifted(): return lax.ppermute(x, axis, pairs)]
    psum x1 -> x0, waiting for transfers between devices: 17.9 us -> none  [per_device(): summed = lax.psum(prods, 'mz')]
    concatenate x3 -> x0, local copies, waits for them, and re-layouts: 11.1 us -> none  [the longest x1 10.5 us: per_device(): jnp.concatenate([padded[:, SPAN - l * LAG:SPAN - l * LAG + total] for l i...]
    ppermute x3 -> x0, starting transfers between devices: 10.7 us -> none  [shifted(): return lax.ppermute(x, axis, pairs)]
  transfers between devices with their start and end apart: 6 -> 0, of which waited for: 4 -> 0; matrix products, arithmetic and copies ran while one was open for 7% -> 0% of each run, Pallas kernels for 0% -> 0%
where the time goes in v1:
time: 205 us; the launch traced here: 204 us
  Pallas kernels  198 us (97%)
  local copies, waits for them, and re-layouts  6.3 us (3%)
    pallas_call x1, Pallas kernels, per_device(): pl.pallas_call(functools.partial(kernel, n, chunks), out_shape=(jax.Shape...  198 us

profile of v1, /device:TPU:0, one launch (start us, length us, event | category | flops | bytes accessed | tf_op | source)
XLA Modules:
  0.0 204.4 jit_solution(10145755085711344053)
XLA Ops:
  0.6 0.7 tile.2
  1.3 0.7 broadcast_in_dim_tile.3.w_rate
  1.9 1.4 copy.7.h_rate
  3.3 197.5 %shard_map.68 = (f32[64,512]{1,0:T(8,128)}, bf16[768,512]{1,0:T(8,128)(2,1)}) custom-call(bf16[6144,512]{1,0:T(8,128)(2,1)} %spectra.1, bf16[768,512]{1,0:T(8,128)(2,1)} %bitcast.5, f32[64,512]{1,0:T(8,128)} %act_ref.1, f32[64,1]{1,0:T(8,128)} %copy.7.h_rate, f32[1,512]{1,0:T(1,128)} %broadcast_in_dim_tile.3.w_rate), custom_call_target="tpu_custom_call" | custom-call | flops 12884901888 | bytes 12582912 | tf_op jit(solution)/shard_map/pallas_call | solution.py:263
  200.8 1.6 copy.10
  202.4 2.1 %copy.11 = bf16[1,768,512]{2,1,0:T(8,128)(2,1)} copy(bf16[1,768,512]{2,1,0:T(8,128)(2,1)} %bitcast.3) | data formatting | bytes 1572864

commit v2 on v1

--- a/solution.py
+++ b/solution.py
@@ -24,10 +24,28 @@
     return out
 
 
+def column(row):
+    shape = (K, K)
+    same = lax.broadcasted_iota(jnp.int32, shape, 0) == lax.broadcasted_iota(jnp.int32, shape, 1)
+    return jnp.sum(jnp.where(same, row, 0.0), axis=1, keepdims=True)
+
+
+def store(h_in, w_in, h_out, w_out, sems):
+    copies = [
+        pltpu.make_async_copy(w_in, w_out, sems.at[0]),
+        pltpu.make_async_copy(h_in, h_out, sems.at[1]),
+    ]
+    for copy in copies:
+        copy.start()
+    for copy in copies:
+        copy.wait()
+
+
 def kernel(
     n, chunks, spectra, w_ref, act_ref, h_rate, w_rate, h_out, w_out,
     sbuf, hraw, stack, gacc, gfin, from_core, gsum, from_scan, nh, hn, total_w,
-    own_sem, s_send, s_recv, h_send, h_recv, a_sem, b_send, b_recv, c_send, c_recv, d_sem, e_sem,
+    own_sem, s_send, s_recv, h_send, h_recv, a_send, a_recv, b_send, b_recv, c_send, c_recv,
+    d_send, d_recv, e_sem,
 ):
     rows, width = sbuf.shape[1], sbuf.shape[2]
     half = width // 2
@@ -69,10 +87,14 @@
             recv_sem=h_recv.at[source(d)], device_id={"scan": to(d)}, device_id_type=MESH,
         )
 
-    def send_s(c, d):
-        return pltpu.make_async_remote_copy(
-            src_ref=spectra.at[pl.ds(pl.multiple_of(to(d) * rows + c * step, step), step), :],
-            dst_ref=sbuf.at[i, pl.ds(c * step, step), :],
+    pieces = 2 if step % 32 == 0 else 1
+    piece = step // pieces
+
+    def send_s(c, u, d):
+        first = c * step + u * piece
+        return pltpu.make_async_remote_copy(
+            src_ref=spectra.at[pl.ds(pl.multiple_of(to(d) * rows + first, piece), piece), :],
+            dst_ref=sbuf.at[i, pl.ds(first, piece), :],
             send_sem=s_send.at[c, d], recv_sem=s_recv.at[c, i],
             device_id={"scan": to(d)}, device_id_type=MESH,
         )
@@ -90,26 +112,25 @@
     )
     own.start()
     each(lambda d: send_h(d).start())
+    turn = (2 * lax.rem(i // 2, 2) + mz) * (n - 1) // 4
     for c in range(chunks):
-        each(lambda e, c=c: send_s(c, n - e).start())
+        for u in range(pieces):
+            each(lambda e, c=c, u=u: send_s(c, u, n - 1 - lax.rem(e - 1 + turn, n - 1)).start())
 
     gacc[...] = jnp.zeros_like(gacc)
     each(lambda d: land_h(d).wait_recv())
 
-    def build(block):
-        def one(j):
-            now = block(j).astype(F32)
-            before = jnp.where(j > 0, block(jnp.maximum(j - 1, 0)).astype(F32), 0.0)
-            ext = jnp.concatenate([before, now], 1)
-            odd = pltpu.roll(ext, LAG, 1)
-            for l in range(LAGS):
-                start = width - LANES * (l // 2)
-                part = (odd if l % 2 else ext)[:, start : start + width]
-                stack[j, l * K : (l + 1) * K, :] = part.astype(BF16)
-
-        each(one, 0)
-
-    build(lambda j: hraw[j])
+    def build(block, j):
+        now = block(j).astype(F32)
+        before = jnp.where(j > 0, block(jnp.maximum(j - 1, 0)).astype(F32), 0.0)
+        ext = jnp.concatenate([before, now], 1)
+        odd = pltpu.roll(ext, LAG, 1)
+        for l in range(LAGS):
+            start = width - LANES * (l // 2)
+            part = (odd if l % 2 else ext)[:, start : start + width]
+            stack[j, l * K : (l + 1) * K, :] = part.astype(BF16)
+
+    each(lambda j: build(lambda b: hraw[b], j), 0)
     own.wait()
 
     def residual(c, j):
@@ -154,19 +175,18 @@
         gfin[0, j] = g[:, :half]
         gfin[1, j] = g[:, half:]
 
-    each(finish, 0)
-
-    a_copy = pltpu.make_async_remote_copy(
-        src_ref=gfin.at[other], dst_ref=from_core, send_sem=a_sem.at[0], recv_sem=a_sem.at[1],
-        device_id={"mz": other}, device_id_type=MESH,
-    )
-    a_copy.start()
-    a_copy.wait_recv()
-
-    def add_core(j):
-        gsum[j] = gfin[mz, j] + from_core[j]
-
-    each(add_core, 0)
+    def core_copy(j):
+        return pltpu.make_async_remote_copy(
+            src_ref=gfin.at[other, j], dst_ref=from_core.at[j], send_sem=a_send.at[j],
+            recv_sem=a_recv.at[j], device_id={"mz": other}, device_id_type=MESH,
+        )
+
+    def finish_and_send(e):
+        j = to(n - 1 - e)
+        finish(j)
+        core_copy(j).start()
+
+    each(finish_and_send, 0)
 
     def send_g(d):
         return pltpu.make_async_remote_copy(
@@ -180,7 +200,16 @@
             recv_sem=b_recv.at[source(d)], device_id={"scan": to(d)}, device_id_type=MESH,
         )
 
-    each(lambda e: send_g(n - e).start())
+    def add_core(j):
+        core_copy(j).wait_recv()
+        gsum[j] = gfin[mz, j] + from_core[j]
+
+    def add_and_send(e):
+        add_core(to(n - e))
+        send_g(n - e).start()
+
+    each(add_and_send)
+    add_core(i)
 
     def add_scan(d, total):
         land_g(d).wait_recv()
@@ -189,67 +218,95 @@
     grad = scale * lax.fori_loop(1, n, add_scan, gsum[i])
     act = act_ref[...]
     act = jnp.where(mz == 0, act[:, :half], act[:, half:])
-    new_h = jnp.maximum(act - h_rate[...] * grad, 0.0)
+    new_h = jnp.maximum(act - column(h_rate[...]) * grad, 0.0)
     nh[mz] = new_h
     hn[mz, i] = new_h.astype(BF16)
 
-    def send_n(d):
-        return pltpu.make_async_remote_copy(
-            src_ref=hn.at[mz, i], dst_ref=hn.at[mz, i], send_sem=c_send.at[d],
-            recv_sem=c_recv.at[i], device_id={"scan": to(d)}, device_id_type=MESH,
-        )
-
-    def land_n(d):
-        return pltpu.make_async_remote_copy(
-            src_ref=hn.at[mz, source(d)], dst_ref=hn.at[mz, source(d)], send_sem=c_send.at[d],
-            recv_sem=c_recv.at[source(d)], device_id={"scan": to(d)}, device_id_type=MESH,
-        )
-
-    each(lambda e: send_n(n - e).start())
+    def after(t):
+        return lax.rem(i + t, n)
+
+    def send_n(t):
+        return pltpu.make_async_remote_copy(
+            src_ref=hn.at[mz, i], dst_ref=hn.at[mz, i], send_sem=c_send.at[t],
+            recv_sem=c_recv.at[i], device_id={"scan": after(n - t)}, device_id_type=MESH,
+        )
+
+    def land_n(t):
+        return pltpu.make_async_remote_copy(
+            src_ref=hn.at[mz, after(t)], dst_ref=hn.at[mz, after(t)], send_sem=c_send.at[t],
+            recv_sem=c_recv.at[after(t)], device_id={"scan": after(n - t)}, device_id_type=MESH,
+        )
+
+    def hand_on(j):
+        return pltpu.make_async_remote_copy(
+            src_ref=hn.at[mz, j], dst_ref=hn.at[mz, j], send_sem=d_send.at[j],
+            recv_sem=d_recv.at[j], device_id={"mz": other}, device_id_type=MESH,
+        )
+
+    def handed(j):
+        return pltpu.make_async_remote_copy(
+            src_ref=hn.at[other, j], dst_ref=hn.at[other, j], send_sem=d_send.at[j],
+            recv_sem=d_recv.at[j], device_id={"mz": other}, device_id_type=MESH,
+        )
+
+    hand_on(i).start()
+    each(lambda t: send_n(t).start())
     e_copy = pltpu.make_async_remote_copy(
         src_ref=nh.at[mz], dst_ref=nh.at[mz], send_sem=e_sem.at[0], recv_sem=e_sem.at[1],
         device_id={"mz": other}, device_id_type=MESH,
     )
     e_copy.start()
-    each(lambda d: land_n(d).wait_recv())
-    d_copy = pltpu.make_async_remote_copy(
-        src_ref=hn.at[mz], dst_ref=hn.at[mz], send_sem=d_sem.at[0], recv_sem=d_sem.at[1],
-        device_id={"mz": other}, device_id_type=MESH,
-    )
-    d_copy.start()
+    total_w[...] = jnp.zeros_like(total_w)
+
+    def take(t):
+        land_n(t).wait_recv()
+        hand_on(after(t)).start()
+
+    take(1)
+    handed(i).wait_recv()
+
+    def second(t, carry):
+        j = after(t)
+
+        @pl.when(t + 1 < n)
+        def _():
+            take(t + 1)
+
+        @pl.when(t < n)
+        def _():
+            handed(j).wait_recv()
+
+        build(lambda b: jnp.concatenate([hn[0, b], hn[1, b]], 1), j)
+        for c in range(chunks):
+            total_w[pl.ds(c * step, step), :] += lax.dot_general(
+                residual(c, j), stack[j], (((1,), (1,)), ((), ())), preferred_element_type=F32
+            )
+        return carry
+
+    lax.fori_loop(1, n + 1, second, 0)
+
+    lags = lax.broadcasted_iota(jnp.int32, (K, LAGS * K), 1)
+    same = lax.rem(lags, K) == lax.broadcasted_iota(jnp.int32, (K, LAGS * K), 0)
+    rates = jnp.sum(jnp.where(same, column(w_rate[...]), 0.0), axis=0, keepdims=True)
+    for c in range(chunks):
+        at = pl.ds(c * step, step)
+        moved = w_ref[at, :].astype(F32) - rates * (scale * total_w[at, :])
+        w_out[at, :] = jnp.maximum(moved, 0.0).astype(BF16)
+
     e_back = pltpu.make_async_remote_copy(
         src_ref=nh.at[other], dst_ref=nh.at[other], send_sem=e_sem.at[0], recv_sem=e_sem.at[1],
         device_id={"mz": other}, device_id_type=MESH,
     )
     e_back.wait_recv()
     h_out[...] = jnp.concatenate([nh[0], nh[1]], 1)
-    d_back = pltpu.make_async_remote_copy(
-        src_ref=hn.at[other], dst_ref=hn.at[other], send_sem=d_sem.at[0], recv_sem=d_sem.at[1],
-        device_id={"mz": other}, device_id_type=MESH,
-    )
-    d_back.wait_recv()
-    build(lambda j: jnp.concatenate([hn[0, j], hn[1, j]], 1))
-
-    for c in range(chunks):
-        total_w[...] = jnp.zeros_like(total_w)
-
-        def add_w(j, c=c):
-            total_w[...] += lax.dot_general(
-                residual(c, j), stack[j], (((1,), (1,)), ((), ())), preferred_element_type=F32
-            )
-
-        each(add_w, 0)
-        at = pl.ds(c * step, step)
-        moved = w_ref[at, :].astype(F32) - w_rate[...] * (scale * total_w[...])
-        w_out[at, :] = jnp.maximum(moved, 0.0).astype(BF16)
 
     each(lambda d: send_h(d).wait_send())
     for c in range(chunks):
-        each(lambda d, c=c: send_s(c, d).wait_send())
+        each(lambda d, c=c: land_s(c, d).wait_send())
     each(lambda d: send_g(d).wait_send())
     each(lambda d: send_n(d).wait_send())
-    a_copy.wait_send()
-    d_copy.wait_send()
+    each(lambda j: core_copy(j).wait_send(), 0)
+    each(lambda j: hand_on(j).wait_send(), 0)
     e_copy.wait_send()
 
 
@@ -279,18 +336,20 @@
             pltpu.VMEM((n, K, half), F32),
             pltpu.VMEM((2, K, half), F32),
             pltpu.VMEM((2, n, K, half), BF16),
-            pltpu.VMEM((rows // chunks, cols), F32),
+            pltpu.VMEM((rows, cols), F32),
             dma,
             dma((chunks, n)),
             dma((chunks, n)),
             dma((n,)),
             dma((n,)),
-            dma((2,)),
-            dma((n,)),
-            dma((n,)),
-            dma((n,)),
-            dma((n,)),
-            dma((2,)),
+            dma((n,)),
+            dma((n,)),
+            dma((n,)),
+            dma((n,)),
+            dma((n,)),
+            dma((n,)),
+            dma((n,)),
+            dma((n,)),
             dma((2,)),
         ],
         compiler_params=pltpu.CompilerParams(
@@ -303,9 +362,20 @@
         spectra,
         templates.reshape(rows, cols),
         activations,
-        h_rate[:, None],
-        jnp.tile(w_rate, LAGS)[None, :],
-    )
+        h_rate.reshape(1, K),
+        w_rate.reshape(1, K),
+    )
+    hbm = pl.BlockSpec(memory_space=pltpu.HBM)
+    new_h, new_w = pl.pallas_call(
+        store,
+        out_shape=(
+            jax.ShapeDtypeStruct(new_h.shape, F32),
+            jax.ShapeDtypeStruct(new_w.shape, BF16),
+        ),
+        in_specs=[hbm, hbm],
+        out_specs=(hbm, hbm),
+        scratch_shapes=[dma((2,))],
+    )(new_h, new_w)
     return new_h, new_w.reshape(templates.shape)
 
 

time: 205 us -> 217 us (1.059)
  Pallas kernels: 198 us -> 216 us
  local copies, waits for them, and re-layouts: 6.3 us -> 0 us
    pallas_call x0 -> x1, Pallas kernels: none -> 28.9 us  [per_device(): pl.pallas_call(store, out_shape=(jax.ShapeDtypeStruct(new_h.shape, F32),...]
    pallas_call x1, Pallas kernels: 198 us -> 187 us  [per_device(): pl.pallas_call(functools.partial(kernel, n, chunks), out_shape=(jax.Shape...]
    unnamed x2 -> x0, local copies, waits for them, and re-layouts: 3.63 us -> none
where the time goes in v2:
time: 217 us
  Pallas kernels  216 us (100%)
    pallas_call x1, Pallas kernels, per_device(): pl.pallas_call(functools.partial(kernel, n, chunks), out_shape=(jax.Shape...  187 us
    pallas_call x1, Pallas kernels, per_device(): pl.pallas_call(store, out_shape=(jax.ShapeDtypeStruct(new_h.shape, F32),...  28.9 us

profile of v2, /device:TPU:0, one launch (start us, length us, event | category | flops | bytes accessed | tf_op | source)
XLA Modules:
  0.0 216.6 jit_solution(5395607643060867710)
XLA Ops:
  0.6 187.0 %shard_map.68 = (f32[64,512]{1,0:T(8,128)}, bf16[768,512]{1,0:T(8,128)(2,1)}) custom-call(bf16[6144,512]{1,0:T(8,128)(2,1)} %spectra.1, bf16[768,512]{1,0:T(8,128)(2,1)} %bitcast.4, f32[64,512]{1,0:T(8,128)} %act_ref.1, f32[1,64]{1,0:T(1,128)} %bitcast.6, f32[1,64]{1,0:T(1,128)} %bitcast.7), custom_call_target="tpu_custom_call" | custom-call | flops 12884901888 | bytes 12582912 | tf_op jit(solution)/shard_map/pallas_call | solution.py:320
  187.7 28.9 %shard_map.69 = (f32[64,512]{1,0:T(8,128)}, bf16[768,512]{1,0:T(8,128)(2,1)}) custom-call(f32[64,512]{1,0:T(8,128)} %get-tuple-element.6.h_in, bf16[768,512]{1,0:T(8,128)(2,1)} %get-tuple-element.7.w_in), custom_call_target="tpu_custom_call" | custom-call | tf_op jit(solution)/shard_map/pallas_call | solution.py:369

commit v3 on v2

--- a/solution.py
+++ b/solution.py
@@ -30,20 +30,9 @@
     return jnp.sum(jnp.where(same, row, 0.0), axis=1, keepdims=True)
 
 
-def store(h_in, w_in, h_out, w_out, sems):
-    copies = [
-        pltpu.make_async_copy(w_in, w_out, sems.at[0]),
-        pltpu.make_async_copy(h_in, h_out, sems.at[1]),
-    ]
-    for copy in copies:
-        copy.start()
-    for copy in copies:
-        copy.wait()
-
-
 def kernel(
     n, chunks, spectra, w_ref, act_ref, h_rate, w_rate, h_out, w_out,
-    sbuf, hraw, stack, gacc, gfin, from_core, gsum, from_scan, nh, hn, total_w,
+    sbuf, hraw, stack, gacc, gfin, from_core, gsum, from_scan, nh, hn, total_w, w_across,
     own_sem, s_send, s_recv, h_send, h_recv, a_send, a_recv, b_send, b_recv, c_send, c_recv,
     d_send, d_recv, e_sem,
 ):
@@ -99,6 +88,25 @@
             device_id={"scan": to(d)}, device_id_type=MESH,
         )
 
+    def send_last(u, t):
+        p = lax.rem(i + t, n)
+        first = (chunks - 1) * step + u * piece
+        return pltpu.make_async_remote_copy(
+            src_ref=spectra.at[pl.ds(pl.multiple_of(p * rows + first, piece), piece), :],
+            dst_ref=sbuf.at[i, pl.ds(first, piece), :],
+            send_sem=s_send.at[chunks - 1, t], recv_sem=s_recv.at[chunks - 1, i],
+            device_id={"scan": p}, device_id_type=MESH,
+        )
+
+    def land_last(t):
+        j = lax.rem(i + n - t, n)
+        at = pl.ds((chunks - 1) * step, step)
+        return pltpu.make_async_remote_copy(
+            src_ref=spectra.at[at, :], dst_ref=sbuf.at[j, at, :],
+            send_sem=s_send.at[chunks - 1, t], recv_sem=s_recv.at[chunks - 1, j],
+            device_id={"scan": lax.rem(i + t, n)}, device_id_type=MESH,
+        )
+
     def land_s(c, d):
         return pltpu.make_async_remote_copy(
             src_ref=spectra.at[pl.ds(c * step, step), :],
@@ -115,9 +123,12 @@
     turn = (2 * lax.rem(i // 2, 2) + mz) * (n - 1) // 4
     for c in range(chunks):
         for u in range(pieces):
-            each(lambda e, c=c, u=u: send_s(c, u, n - 1 - lax.rem(e - 1 + turn, n - 1)).start())
+            if c < chunks - 1:
+                each(lambda e, c=c, u=u: send_s(c, u, n - 1 - lax.rem(e - 1 + turn, n - 1)).start())
+    each(lambda t: [send_last(u, t).start() for u in range(pieces)])
 
     gacc[...] = jnp.zeros_like(gacc)
+    w_across[...] = w_ref[...].T
     each(lambda d: land_h(d).wait_recv())
 
     def build(block, j):
@@ -128,7 +139,7 @@
         for l in range(LAGS):
             start = width - LANES * (l // 2)
             part = (odd if l % 2 else ext)[:, start : start + width]
-            stack[j, l * K : (l + 1) * K, :] = part.astype(BF16)
+            stack[j, l * K : (l + 1) * K, :] = (scale * part).astype(BF16)
 
     each(lambda j: build(lambda b: hraw[b], j), 0)
     own.wait()
@@ -136,14 +147,13 @@
     def residual(c, j):
         at = pl.ds(c * step, step)
         recon = jnp.dot(w_ref[at, :], stack[j], preferred_element_type=F32)
-        return (scale * recon - sbuf[j, at, :].astype(F32)).astype(BF16)
+        return (recon - sbuf[j, at, :].astype(F32)).astype(BF16)
 
     groups = width // LANES
 
     def unit(c, j):
-        prods = lax.dot_general(
-            w_ref[pl.ds(c * step, step), :], residual(c, j), (((0,), (0,)), ((), ())),
-            preferred_element_type=F32,
+        prods = jnp.dot(
+            w_across[:, c * step : (c + 1) * step], residual(c, j), preferred_element_type=F32
         )
         for odd in range(2):
             for q in range(1 - groups, groups):
@@ -160,7 +170,7 @@
                 at = (q % groups) * LANES
                 gacc[odd, block, :, at : at + LANES] += functools.reduce(lambda a, b: a + b, terms)
 
-    for c in range(chunks):
+    for c in range(chunks - 1):
         unit(c, i)
 
         def arrived(d, c=c):
@@ -181,39 +191,50 @@
             recv_sem=a_recv.at[j], device_id={"mz": other}, device_id_type=MESH,
         )
 
-    def finish_and_send(e):
-        j = to(n - 1 - e)
-        finish(j)
-        core_copy(j).start()
-
-    each(finish_and_send, 0)
-
-    def send_g(d):
-        return pltpu.make_async_remote_copy(
-            src_ref=gsum.at[to(d)], dst_ref=from_scan.at[i], send_sem=b_send.at[d],
-            recv_sem=b_recv.at[i], device_id={"scan": to(d)}, device_id_type=MESH,
-        )
-
-    def land_g(d):
-        return pltpu.make_async_remote_copy(
-            src_ref=gsum.at[to(d)], dst_ref=from_scan.at[source(d)], send_sem=b_send.at[d],
-            recv_sem=b_recv.at[source(d)], device_id={"scan": to(d)}, device_id_type=MESH,
+    def send_g(j):
+        return pltpu.make_async_remote_copy(
+            src_ref=gsum.at[j], dst_ref=from_scan.at[i], send_sem=b_send.at[j],
+            recv_sem=b_recv.at[i], device_id={"scan": j}, device_id_type=MESH,
+        )
+
+    def land_g(j):
+        return pltpu.make_async_remote_copy(
+            src_ref=gsum.at[j], dst_ref=from_scan.at[j], send_sem=b_send.at[j],
+            recv_sem=b_recv.at[j], device_id={"scan": j}, device_id_type=MESH,
         )
 
     def add_core(j):
         core_copy(j).wait_recv()
         gsum[j] = gfin[mz, j] + from_core[j]
 
-    def add_and_send(e):
-        add_core(to(n - e))
-        send_g(n - e).start()
-
-    each(add_and_send)
+    def add_and_send(t):
+        j = lax.rem(i + n - t, n)
+        add_core(j)
+        send_g(j).start()
+
+    unit(chunks - 1, i)
+
+    def last(t):
+        j = lax.rem(i + n - t, n)
+        land_last(t).wait_recv()
+        unit(chunks - 1, j)
+        finish(j)
+        core_copy(j).start()
+
+        @pl.when(t > 1)
+        def _():
+            add_and_send(t - 1)
+
+    each(last)
+    finish(i)
+    core_copy(i).start()
+    add_and_send(n - 1)
     add_core(i)
 
     def add_scan(d, total):
-        land_g(d).wait_recv()
-        return total + from_scan[source(d)]
+        j = lax.rem(i + d, n)
+        land_g(j).wait_recv()
+        return total + from_scan[j]
 
     grad = scale * lax.fori_loop(1, n, add_scan, gsum[i])
     act = act_ref[...]
@@ -290,8 +311,8 @@
     rates = jnp.sum(jnp.where(same, column(w_rate[...]), 0.0), axis=0, keepdims=True)
     for c in range(chunks):
         at = pl.ds(c * step, step)
-        moved = w_ref[at, :].astype(F32) - rates * (scale * total_w[at, :])
-        w_out[at, :] = jnp.maximum(moved, 0.0).astype(BF16)
+        moved = w_ref[at, :].astype(F32) - rates * total_w[at, :]
+        w_out[at, :] = moved.astype(BF16)
 
     e_back = pltpu.make_async_remote_copy(
         src_ref=nh.at[other], dst_ref=nh.at[other], send_sem=e_sem.at[0], recv_sem=e_sem.at[1],
@@ -303,7 +324,7 @@
     each(lambda d: send_h(d).wait_send())
     for c in range(chunks):
         each(lambda d, c=c: land_s(c, d).wait_send())
-    each(lambda d: send_g(d).wait_send())
+    each(lambda t: send_g(lax.rem(i + t, n)).wait_send())
     each(lambda d: send_n(d).wait_send())
     each(lambda j: core_copy(j).wait_send(), 0)
     each(lambda j: hand_on(j).wait_send(), 0)
@@ -337,6 +358,7 @@
             pltpu.VMEM((2, K, half), F32),
             pltpu.VMEM((2, n, K, half), BF16),
             pltpu.VMEM((rows, cols), F32),
+            pltpu.VMEM((cols, rows), BF16),
             dma,
             dma((chunks, n)),
             dma((chunks, n)),
@@ -365,17 +387,8 @@
         h_rate.reshape(1, K),
         w_rate.reshape(1, K),
     )
-    hbm = pl.BlockSpec(memory_space=pltpu.HBM)
-    new_h, new_w = pl.pallas_call(
-        store,
-        out_shape=(
-            jax.ShapeDtypeStruct(new_h.shape, F32),
-            jax.ShapeDtypeStruct(new_w.shape, BF16),
-        ),
-        in_specs=[hbm, hbm],
-        out_specs=(hbm, hbm),
-        scratch_shapes=[dma((2,))],
-    )(new_h, new_w)
+    new_h = jnp.maximum(new_h, 0.0)
+    new_w = jnp.maximum(new_w, jnp.zeros((), BF16))
     return new_h, new_w.reshape(templates.shape)
 
 

time: 217 us -> 193 us (0.89)
  Pallas kernels: 216 us -> 188 us
  other arithmetic: 0 us -> 3.63 us
    pallas_call x1 -> x0, Pallas kernels: 28.9 us -> none  [per_device(): pl.pallas_call(store, out_shape=(jax.ShapeDtypeStruct(new_h.shape, F32),...]
where the time goes in v3:
time: 193 us; the launch traced here: 192 us
  Pallas kernels  188 us (97%)
  other arithmetic  3.63 us (2%)
    pallas_call x1, Pallas kernels, per_device(): pl.pallas_call(functools.partial(kernel, n, chunks), out_shape=(jax.Shape...  188 us

profile of v3, /device:TPU:0, one launch (start us, length us, event | category | flops | bytes accessed | tf_op | source)
XLA Modules:
  0.0 192.2 jit_solution(12425673146315560416)
XLA Ops:
  0.6 187.9 %shard_map.68 = (f32[64,512]{1,0:T(8,128)}, bf16[768,512]{1,0:T(8,128)(2,1)}) custom-call(bf16[6144,512]{1,0:T(8,128)(2,1)} %spectra.1, bf16[768,512]{1,0:T(8,128)(2,1)} %bitcast.5, f32[64,512]{1,0:T(8,128)} %act_ref.1, f32[1,64]{1,0:T(1,128)} %bitcast.6, f32[1,64]{1,0:T(1,128)} %bitcast.7), custom_call_target="tpu_custom_call" | custom-call | flops 12884901888 | bytes 12582912 | tf_op jit(solution)/shard_map/pallas_call | solution.py:341
  188.6 1.6 broadcast_maximum_fusion
  190.1 2.1 %maximum_bitcast_fusion = bf16[1,768,512]{2,1,0:T(8,128)(2,1)} fusion(bf16[768,512]{1,0:T(8,128)(2,1)} %get-tuple-element.5), kind=kLoop, calls=%fused_computation | loop fusion | flops 393216 | bytes 1572864 | tf_op jit(solution)/shard_map/reshape | solution.py:392

commit v4 on v3

--- a/solution.py
+++ b/solution.py
@@ -34,7 +34,7 @@
     n, chunks, spectra, w_ref, act_ref, h_rate, w_rate, h_out, w_out,
     sbuf, hraw, stack, gacc, gfin, from_core, gsum, from_scan, nh, hn, total_w, w_across,
     own_sem, s_send, s_recv, h_send, h_recv, a_send, a_recv, b_send, b_recv, c_send, c_recv,
-    d_send, d_recv, e_sem,
+    d_send, d_recv, p_send, f_send, f_recv, e_sem, k_sem, from_pair, q_send,
 ):
     rows, width = sbuf.shape[1], sbuf.shape[2]
     half = width // 2
@@ -58,23 +58,36 @@
 
         lax.fori_loop(start, n, run, 0)
 
+    act = act_ref[...]
+    hraw[0, i] = act[:, :half].astype(BF16)
+    hraw[1, i] = act[:, half:].astype(BF16)
     barrier = pltpu.get_barrier_semaphore()
     each(lambda d: pl.semaphore_signal(barrier, inc=1, device_id={"scan": to(d)}, device_id_type=MESH))
     pl.semaphore_signal(barrier, inc=1, device_id={"mz": other}, device_id_type=MESH)
-    hraw[i] = act_ref[...].astype(BF16)
+    pair = i + 1 - 2 * lax.rem(i, 2)
     pl.semaphore_wait(barrier, n)
 
-    def send_h(d):
-        return pltpu.make_async_remote_copy(
-            src_ref=hraw.at[i], dst_ref=hraw.at[i], send_sem=h_send.at[d], recv_sem=h_recv.at[i],
-            device_id={"scan": to(d)}, device_id_type=MESH,
-        )
-
-    def land_h(d):
-        return pltpu.make_async_remote_copy(
-            src_ref=hraw.at[source(d)], dst_ref=hraw.at[source(d)], send_sem=h_send.at[d],
-            recv_sem=h_recv.at[source(d)], device_id={"scan": to(d)}, device_id_type=MESH,
-        )
+    def along(t):
+        return lax.rem(i + t, n)
+
+    def column_copy(ref, sends, lands, t, j):
+        return pltpu.make_async_remote_copy(
+            src_ref=ref.at[mz, j], dst_ref=ref.at[mz, j], send_sem=sends.at[t],
+            recv_sem=lands.at[j], device_id={"scan": along(n - t)}, device_id_type=MESH,
+        )
+
+    def pair_copy(ref, sends, lands, j):
+        return pltpu.make_async_remote_copy(
+            src_ref=ref.at[mz, j], dst_ref=ref.at[mz, j], send_sem=sends.at[j],
+            recv_sem=lands.at[j], device_id={"scan": pair}, device_id_type=MESH,
+        )
+
+    def evens(body):
+        def run(t, carry):
+            body(2 * t)
+            return carry
+
+        lax.fori_loop(1, n // 2, run, 0)
 
     pieces = 2 if step % 32 == 0 else 1
     piece = step // pieces
@@ -119,9 +132,24 @@
         spectra.at[pl.ds(pl.multiple_of(i * rows, rows), rows), :], sbuf.at[i], own_sem
     )
     own.start()
-    each(lambda d: send_h(d).start())
+    pair_copy(hraw, p_send, h_recv, i).start()
+    evens(lambda t: column_copy(hraw, h_send, h_recv, t, i).start())
     turn = (2 * lax.rem(i // 2, 2) + mz) * (n - 1) // 4
+
+    def pass_on(t):
+        j = along(t)
+        column_copy(hraw, h_send, h_recv, t, j).wait_recv()
+        pair_copy(hraw, p_send, h_recv, j).start()
+
+    def core_halves(h):
+        return pltpu.make_async_remote_copy(
+            src_ref=hraw.at[h], dst_ref=hraw.at[h], send_sem=k_sem.at[0], recv_sem=k_sem.at[1],
+            device_id={"mz": other}, device_id_type=MESH,
+        )
+
     for c in range(chunks):
+        if c == min(1, chunks - 1):
+            evens(pass_on)
         for u in range(pieces):
             if c < chunks - 1:
                 each(lambda e, c=c, u=u: send_s(c, u, n - 1 - lax.rem(e - 1 + turn, n - 1)).start())
@@ -129,7 +157,13 @@
 
     gacc[...] = jnp.zeros_like(gacc)
     w_across[...] = w_ref[...].T
-    each(lambda d: land_h(d).wait_recv())
+
+    def from_other_column(t):
+        pair_copy(hraw, p_send, h_recv, along(t)).wait_recv()
+
+    lax.fori_loop(0, n // 2, lambda t, carry: (from_other_column(2 * t + 1), carry)[1], 0)
+    core_halves(mz).start()
+    core_halves(other).wait_recv()
 
     def build(block, j):
         now = block(j).astype(F32)
@@ -141,7 +175,7 @@
             part = (odd if l % 2 else ext)[:, start : start + width]
             stack[j, l * K : (l + 1) * K, :] = (scale * part).astype(BF16)
 
-    each(lambda j: build(lambda b: hraw[b], j), 0)
+    each(lambda j: build(lambda b: jnp.concatenate([hraw[0, b], hraw[1, b]], 1), j), 0)
     own.wait()
 
     def residual(c, j):
@@ -203,14 +237,25 @@
             recv_sem=b_recv.at[j], device_id={"scan": j}, device_id_type=MESH,
         )
 
-    def add_core(j):
+    def pair_sum(j):
+        return pltpu.make_async_remote_copy(
+            src_ref=gsum.at[j], dst_ref=from_pair.at[j], send_sem=f_send.at[j],
+            recv_sem=f_recv.at[j], device_id={"scan": pair}, device_id_type=MESH,
+        )
+
+    def add_core(t):
+        j = along(n - t)
         core_copy(j).wait_recv()
         gsum[j] = gfin[mz, j] + from_core[j]
 
-    def add_and_send(t):
-        j = lax.rem(i + n - t, n)
-        add_core(j)
-        send_g(j).start()
+        @pl.when(lax.rem(t, 2) == 1)
+        def _():
+            pair_sum(j).start()
+
+    def add_pair(t):
+        j = along(n - t)
+        pair_sum(j).wait_recv()
+        gsum[j] = gsum[j] + from_pair[j]
 
     unit(chunks - 1, i)
 
@@ -223,41 +268,33 @@
 
         @pl.when(t > 1)
         def _():
-            add_and_send(t - 1)
+            add_core(t - 1)
+
+        @pl.when(jnp.logical_and(t > 3, lax.rem(t, 2) == 1))
+        def _():
+            add_pair(t - 3)
+            send_g(along(n - t + 3)).start()
 
     each(last)
     finish(i)
     core_copy(i).start()
-    add_and_send(n - 1)
-    add_core(i)
+    add_core(n - 1)
+    add_pair(n - 2)
+    send_g(along(2)).start()
+    add_core(0)
+    add_pair(0)
 
     def add_scan(d, total):
-        j = lax.rem(i + d, n)
+        j = along(2 * d)
         land_g(j).wait_recv()
         return total + from_scan[j]
 
-    grad = scale * lax.fori_loop(1, n, add_scan, gsum[i])
-    act = act_ref[...]
+    grad = scale * lax.fori_loop(1, n // 2, add_scan, gsum[i])
     act = jnp.where(mz == 0, act[:, :half], act[:, half:])
     new_h = jnp.maximum(act - column(h_rate[...]) * grad, 0.0)
     nh[mz] = new_h
     hn[mz, i] = new_h.astype(BF16)
 
-    def after(t):
-        return lax.rem(i + t, n)
-
-    def send_n(t):
-        return pltpu.make_async_remote_copy(
-            src_ref=hn.at[mz, i], dst_ref=hn.at[mz, i], send_sem=c_send.at[t],
-            recv_sem=c_recv.at[i], device_id={"scan": after(n - t)}, device_id_type=MESH,
-        )
-
-    def land_n(t):
-        return pltpu.make_async_remote_copy(
-            src_ref=hn.at[mz, after(t)], dst_ref=hn.at[mz, after(t)], send_sem=c_send.at[t],
-            recv_sem=c_recv.at[after(t)], device_id={"scan": after(n - t)}, device_id_type=MESH,
-        )
-
     def hand_on(j):
         return pltpu.make_async_remote_copy(
             src_ref=hn.at[mz, j], dst_ref=hn.at[mz, j], send_sem=d_send.at[j],
@@ -271,7 +308,8 @@
         )
 
     hand_on(i).start()
-    each(lambda t: send_n(t).start())
+    pair_copy(hn, q_send, c_recv, i).start()
+    evens(lambda t: column_copy(hn, c_send, c_recv, t, i).start())
     e_copy = pltpu.make_async_remote_copy(
         src_ref=nh.at[mz], dst_ref=nh.at[mz], send_sem=e_sem.at[0], recv_sem=e_sem.at[1],
         device_id={"mz": other}, device_id_type=MESH,
@@ -280,14 +318,19 @@
     total_w[...] = jnp.zeros_like(total_w)
 
     def take(t):
-        land_n(t).wait_recv()
-        hand_on(after(t)).start()
+        j = along(t)
+        pair_copy(hn, q_send, c_recv, j).wait_recv()
+        hand_on(j).start()
+
+        @pl.when(lax.rem(t, 2) == 0)
+        def _():
+            pair_copy(hn, q_send, c_recv, j).start()
 
     take(1)
     handed(i).wait_recv()
 
     def second(t, carry):
-        j = after(t)
+        j = along(t)
 
         @pl.when(t + 1 < n)
         def _():
@@ -321,11 +364,19 @@
     e_back.wait_recv()
     h_out[...] = jnp.concatenate([nh[0], nh[1]], 1)
 
-    each(lambda d: send_h(d).wait_send())
+    evens(lambda t: column_copy(hraw, h_send, h_recv, t, i).wait_send())
+    evens(lambda t: column_copy(hn, c_send, c_recv, t, i).wait_send())
+
+    def own_column(t):
+        pair_copy(hraw, p_send, h_recv, along(2 * t)).wait_send()
+        pair_copy(hn, q_send, c_recv, along(2 * t)).wait_send()
+        pair_sum(along(2 * t + 1)).wait_send()
+
+    lax.fori_loop(0, n // 2, lambda t, carry: (own_column(t), carry)[1], 0)
+    core_halves(mz).wait_send()
     for c in range(chunks):
         each(lambda d, c=c: land_s(c, d).wait_send())
-    each(lambda t: send_g(lax.rem(i + t, n)).wait_send())
-    each(lambda d: send_n(d).wait_send())
+    evens(lambda t: send_g(along(t)).wait_send())
     each(lambda j: core_copy(j).wait_send(), 0)
     each(lambda j: hand_on(j).wait_send(), 0)
     e_copy.wait_send()
@@ -348,7 +399,7 @@
         out_specs=(vmem, vmem),
         scratch_shapes=[
             pltpu.VMEM((n, rows, width), BF16),
-            pltpu.VMEM((n, K, width), BF16),
+            pltpu.VMEM((2, n, K, half), BF16),
             pltpu.VMEM((n, cols, width), BF16),
             pltpu.VMEM((2, n + 2, K, width), F32),
             pltpu.VMEM((2, n, K, half), F32),
@@ -372,7 +423,13 @@
             dma((n,)),
             dma((n,)),
             dma((n,)),
+            dma((n,)),
+            dma((n,)),
+            dma((n,)),
             dma((2,)),
+            dma((2,)),
+            pltpu.VMEM((n, K, half), F32),
+            dma((n,)),
         ],
         compiler_params=pltpu.CompilerParams(
             collective_id=0, has_side_effects=True, vmem_limit_bytes=56 * 1024 * 1024

time: 193 us -> 198 us (1.026)
  Pallas kernels: 188 us -> 194 us
    pallas_call x1, Pallas kernels: 188 us -> 194 us  [per_device(): pl.pallas_call(functools.partial(kernel, n, chunks), out_shape=(jax.Shape...]
where the time goes in v4:
time: 198 us
  Pallas kernels  194 us (98%)
  other arithmetic  3.63 us (2%)
    pallas_call x1, Pallas kernels, per_device(): pl.pallas_call(functools.partial(kernel, n, chunks), out_shape=(jax.Shape...  194 us

profile of v4, /device:TPU:0, one launch (start us, length us, event | category | flops | bytes accessed | tf_op | source)
XLA Modules:
  0.0 198.1 jit_solution(15978444749144320351)
XLA Ops:
  0.6 193.8 %shard_map.68 = (f32[64,512]{1,0:T(8,128)}, bf16[768,512]{1,0:T(8,128)(2,1)}) custom-call(bf16[6144,512]{1,0:T(8,128)(2,1)} %spectra.1, bf16[768,512]{1,0:T(8,128)(2,1)} %bitcast.5, f32[64,512]{1,0:T(8,128)} %act_ref.1, f32[1,64]{1,0:T(1,128)} %bitcast.6, f32[1,64]{1,0:T(1,128)} %bitcast.7), custom_call_target="tpu_custom_call" | custom-call | flops 12884901888 | bytes 12582912 | tf_op jit(solution)/shard_map/pallas_call | solution.py:392
  194.5 1.6 broadcast_maximum_fusion
  196.0 2.1 %maximum_bitcast_fusion = bf16[1,768,512]{2,1,0:T(8,128)(2,1)} fusion(bf16[768,512]{1,0:T(8,128)(2,1)} %get-tuple-element.5), kind=kLoop, calls=%fused_computation | loop fusion | flops 393216 | bytes 1572864 | tf_op jit(solution)/shard_map/reshape | solution.py:449

commit v5 on v3

--- a/solution.py
+++ b/solution.py
@@ -34,7 +34,7 @@
     n, chunks, spectra, w_ref, act_ref, h_rate, w_rate, h_out, w_out,
     sbuf, hraw, stack, gacc, gfin, from_core, gsum, from_scan, nh, hn, total_w, w_across,
     own_sem, s_send, s_recv, h_send, h_recv, a_send, a_recv, b_send, b_recv, c_send, c_recv,
-    d_send, d_recv, e_sem,
+    d_send, d_recv, e_sem, k_sem,
 ):
     rows, width = sbuf.shape[1], sbuf.shape[2]
     half = width // 2
@@ -58,21 +58,23 @@
 
         lax.fori_loop(start, n, run, 0)
 
+    act = act_ref[...]
+    hraw[0, i] = act[:, :half].astype(BF16)
+    hraw[1, i] = act[:, half:].astype(BF16)
     barrier = pltpu.get_barrier_semaphore()
     each(lambda d: pl.semaphore_signal(barrier, inc=1, device_id={"scan": to(d)}, device_id_type=MESH))
     pl.semaphore_signal(barrier, inc=1, device_id={"mz": other}, device_id_type=MESH)
-    hraw[i] = act_ref[...].astype(BF16)
     pl.semaphore_wait(barrier, n)
 
     def send_h(d):
         return pltpu.make_async_remote_copy(
-            src_ref=hraw.at[i], dst_ref=hraw.at[i], send_sem=h_send.at[d], recv_sem=h_recv.at[i],
+            src_ref=hraw.at[mz, i], dst_ref=hraw.at[mz, i], send_sem=h_send.at[d], recv_sem=h_recv.at[i],
             device_id={"scan": to(d)}, device_id_type=MESH,
         )
 
     def land_h(d):
         return pltpu.make_async_remote_copy(
-            src_ref=hraw.at[source(d)], dst_ref=hraw.at[source(d)], send_sem=h_send.at[d],
+            src_ref=hraw.at[mz, source(d)], dst_ref=hraw.at[mz, source(d)], send_sem=h_send.at[d],
             recv_sem=h_recv.at[source(d)], device_id={"scan": to(d)}, device_id_type=MESH,
         )
 
@@ -130,6 +132,15 @@
     gacc[...] = jnp.zeros_like(gacc)
     w_across[...] = w_ref[...].T
     each(lambda d: land_h(d).wait_recv())
+
+    def core_halves(h):
+        return pltpu.make_async_remote_copy(
+            src_ref=hraw.at[h], dst_ref=hraw.at[h], send_sem=k_sem.at[0], recv_sem=k_sem.at[1],
+            device_id={"mz": other}, device_id_type=MESH,
+        )
+
+    core_halves(mz).start()
+    core_halves(other).wait_recv()
 
     def build(block, j):
         now = block(j).astype(F32)
@@ -141,7 +152,7 @@
             part = (odd if l % 2 else ext)[:, start : start + width]
             stack[j, l * K : (l + 1) * K, :] = (scale * part).astype(BF16)
 
-    each(lambda j: build(lambda b: hraw[b], j), 0)
+    each(lambda j: build(lambda b: jnp.concatenate([hraw[0, b], hraw[1, b]], 1), j), 0)
     own.wait()
 
     def residual(c, j):
@@ -237,7 +248,6 @@
         return total + from_scan[j]
 
     grad = scale * lax.fori_loop(1, n, add_scan, gsum[i])
-    act = act_ref[...]
     act = jnp.where(mz == 0, act[:, :half], act[:, half:])
     new_h = jnp.maximum(act - column(h_rate[...]) * grad, 0.0)
     nh[mz] = new_h
@@ -322,6 +332,7 @@
     h_out[...] = jnp.concatenate([nh[0], nh[1]], 1)
 
     each(lambda d: send_h(d).wait_send())
+    core_halves(mz).wait_send()
     for c in range(chunks):
         each(lambda d, c=c: land_s(c, d).wait_send())
     each(lambda t: send_g(lax.rem(i + t, n)).wait_send())
@@ -348,7 +359,7 @@
         out_specs=(vmem, vmem),
         scratch_shapes=[
             pltpu.VMEM((n, rows, width), BF16),
-            pltpu.VMEM((n, K, width), BF16),
+            pltpu.VMEM((2, n, K, half), BF16),
             pltpu.VMEM((n, cols, width), BF16),
             pltpu.VMEM((2, n + 2, K, width), F32),
             pltpu.VMEM((2, n, K, half), F32),
@@ -372,6 +383,7 @@
             dma((n,)),
             dma((n,)),
             dma((n,)),
+            dma((2,)),
             dma((2,)),
         ],
         compiler_params=pltpu.CompilerParams(

time: 193 us -> 187 us (0.969)
  Pallas kernels: 188 us -> 182 us
    pallas_call x1, Pallas kernels: 188 us -> 182 us  [per_device(): pl.pallas_call(functools.partial(kernel, n, chunks), out_shape=(jax.Shape...]
where the time goes in v5:
time: 187 us
  Pallas kernels  182 us (97%)
  other arithmetic  3.63 us (2%)
    pallas_call x1, Pallas kernels, per_device(): pl.pallas_call(functools.partial(kernel, n, chunks), out_shape=(jax.Shape...  182 us

profile of v5, /device:TPU:0, one launch (start us, length us, event | category | flops | bytes accessed | tf_op | source)
XLA Modules:
  0.0 186.7 jit_solution(2733625382323242118)
XLA Ops:
  0.6 182.5 %shard_map.68 = (f32[64,512]{1,0:T(8,128)}, bf16[768,512]{1,0:T(8,128)(2,1)}) custom-call(bf16[6144,512]{1,0:T(8,128)(2,1)} %spectra.1, bf16[768,512]{1,0:T(8,128)(2,1)} %bitcast.5, f32[64,512]{1,0:T(8,128)} %act_ref.1, f32[1,64]{1,0:T(1,128)} %bitcast.6, f32[1,64]{1,0:T(1,128)} %bitcast.7), custom_call_target="tpu_custom_call" | custom-call | flops 12884901888 | bytes 12582912 | tf_op jit(solution)/shard_map/pallas_call | solution.py:352
  183.1 1.6 broadcast_maximum_fusion
  184.7 2.1 %maximum_bitcast_fusion = bf16[1,768,512]{2,1,0:T(8,128)(2,1)} fusion(bf16[768,512]{1,0:T(8,128)(2,1)} %get-tuple-element.5), kind=kLoop, calls=%fused_computation | loop fusion | flops 393216 | bytes 1572864 | tf_op jit(solution)/shard_map/reshape | solution.py:404
